TPU v7x, 128 devices: a whole 4x4x4 slice. The times are simulated.
128 devices in a mesh: gx: 8 (over x, core), row: 16 (over y, z).
Axes of the slice: x: 4, y: 4, z: 4, core: 2. Of those that a mesh axis runs over, the one named last changes fastest.
Arguments:
- eddy_fields: float32 [5, 64, 512, 256], P(None, 'gx', 'row'), may hold values from -0.6 to 0.6, as said below
- acoustic_fields: float32 [4, 128, 256, 256], P(None, 'gx', 'row'), may hold values from -1.2 to 1.2
- weights: bfloat16 [8, 16, 128, 128, 128], P('gx', 'row'), may hold values from -0.5 to 0.5
- source_block: int32 [8, 16, 128], P('gx', 'row'), may hold values from 0 to 511
- target_device: int32 [8, 16, 128, 1], P('gx', 'row'), may hold values from 0 to 127; in each aligned block of 128 rows (0 to 127, 128 to 255, ..., all dimensions but the last counted through in order) at most 2 rows name the same one
- target_block: int32 [8, 16, 128], P('gx', 'row'), may hold values from 0 to 511
- live_count: int32 [8, 16], P('gx', 'row'), may hold values from 64 to 128, as said below
Outputs:
- eddy_next: float32 [5, 64, 512, 256], P(None, 'gx', 'row')
- acoustic_next: float32 [4, 128, 256, 256], P(None, 'gx', 'row')
Inputs may be any that keep to these rules, and one draw needn't show every extreme that they name: `eddy_fields`: channel 0 (density excess) lies within -0.2 to 0.2; the other channels within -0.6 to 0.6. `target_device`: at most 2 of a device's 128 listed entries name one target device, and some device reaches that. `live_count`: at least half of each list is live, and some device has all 128 live.
All inputs are finite; a program needn't handle non-finite values.
Results may differ from a plain program's by a relative error of at most 0.0003.
Values sent between devices are 32-bit elements; how exact they have to be, the bound alone decides.
A program may use at most 192 MiB of HBM per device.

v0:
```python
import functools

import jax
import jax.numpy as jnp
from jax import lax
from jax.experimental import pallas as pl
from jax.experimental.pallas import tpu as pltpu
from jax.sharding import PartitionSpec as P

MESH = pl.DeviceIdType.MESH
F32 = jnp.float32

gamma_gas = 1.4
sound_timestep = 0.5
mean_mach = 0.3
stencil = (0.75, -0.15, 1.0 / 60.0)

GX = 8
ROW = 16
DEV = GX * ROW
FR = 48
AR = 32
CORNERS = ((0, 0), (0, 1), (1, 0), (1, 1))
RADIAL = (0, 2)


def shifted(low, high, lane, step):
    if step > 0:
        a, b = pltpu.roll(low, 128 - step, 1), pltpu.roll(high, 128 - step, 1)
        keep = lane < 128 - step
    else:
        a, b = pltpu.roll(low, -step, 1), pltpu.roll(high, -step, 1)
        keep = lane >= -step
    return jnp.where(keep, a, b), jnp.where(keep, b, a)


def flow_tile(src, x, row, lane, emit):
    rows = pl.ds(row, 8)
    center = [[src[c, x, zh, rows, :] for zh in range(2)] for c in range(5)]
    upper = [shifted(center[c][0], center[c][1], lane, 1) for c in range(5)]
    lower = [shifted(center[c][0], center[c][1], lane, -1) for c in range(5)]
    for zh in range(2):
        dx, dr, dz, lap = [], [], [], []
        for c in range(5):
            xp, xm = src[c, x + 1, zh, rows, :], src[c, x - 1, zh, rows, :]
            rp, rm = src[c, x, zh, pl.ds(row + 1, 8), :], src[c, x, zh, pl.ds(row - 1, 8), :]
            zp, zm = upper[c][zh], lower[c][zh]
            dx.append(xp - xm)
            dr.append(rp - rm)
            dz.append(zp - zm)
            lap.append(((xp + xm) + (rp + rm)) + ((zp + zm) - 6.0 * center[c][zh]))
        q = [center[c][zh] for c in range(5)]
        div = dx[1] + dr[2] + dz[3]
        rho = 1.0 + q[0]
        inv = 1.0 / rho
        force = (
            rho * div,
            dx[4] * inv,
            dr[4] * inv,
            dz[4] * inv,
            (gamma_gas * q[4] + 1.0) * div,
        )
        new = []
        for c in range(5):
            adv = q[1] * dx[c] + q[2] * dr[c] + q[3] * dz[c]
            new.append(q[c] + 0.1 * (lap[c] - adv - force[c]))
        emit(zh, new)


def rate_tile(src, x, row, lane):
    rows = pl.ds(row, 8)

    def grad_x(c, zh):
        total = None
        for k in range(3):
            part = stencil[k] * (src[c, x + 4 + k, zh, rows, :] - src[c, x + 2 - k, zh, rows, :])
            total = part if total is None else total + part
        return total

    def grad_r(c, zh):
        total = None
        for k in range(3):
            part = stencil[k] * (
                src[c, x + 3, zh, pl.ds(row + k + 1, 8), :]
                - src[c, x + 3, zh, pl.ds(row - k - 1, 8), :]
            )
            total = part if total is None else total + part
        return total

    def grad_z(c):
        low, high = src[c, x + 3, 0, rows, :], src[c, x + 3, 1, rows, :]
        total = None
        for k in range(3):
            up = shifted(low, high, lane, k + 1)
            down = shifted(low, high, lane, -k - 1)
            part = [stencil[k] * (up[zh] - down[zh]) for zh in range(2)]
            total = part if total is None else [total[zh] + part[zh] for zh in range(2)]
        return total

    zp, zw = grad_z(0), grad_z(3)
    out = []
    for zh in range(2):
        xp, xu, xv, xw = (grad_x(c, zh) for c in range(4))
        out.append(
            (
                -(mean_mach * xp + xu + grad_r(2, zh) + zw[zh]),
                -(mean_mach * xu + xp),
                -(mean_mach * xv + grad_r(0, zh)),
                -(mean_mach * xw + zp[zh]),
            )
        )
    return out


def kernel(
    eddy, acoustic, weights, target, tblock, sblock, live, eddy_out, acoustic_out,
    f0, f1, f2, srcs, wv, contrib, outgoing, incoming, ys, rsend, rrecv, fsend, frecv, csend, crecv,
    lists, square, turned, slots, slots_s, onehot, source, base, final,
    load_sem, slot_sem, fx_s, fx_r, fr_s, fr_r, fc_s, fc_r, l1_s, l1_r, l2_s, l2_r, aa_s, aa_r,
    ax_s, ax_r, ar_s, ar_r, out_sem,
):
    g, r = lax.axis_index("gx"), lax.axis_index("row")
    me = g * ROW + r
    left, right = lax.rem(g + GX - 1, GX), lax.rem(g + 1, GX)
    below, above = lax.rem(r + ROW - 1, ROW), lax.rem(r + 1, ROW)
    lane = lax.broadcasted_iota(jnp.int32, (8, 128), 1)
    sub = lax.broadcasted_iota(jnp.int32, (8, 128), 0)

    def remote(src, dst, send, recv, where):
        return pltpu.make_async_remote_copy(
            src_ref=src, dst_ref=dst, send_sem=send, recv_sem=recv, device_id=where, device_id_type=MESH
        )

    bar = pltpu.get_barrier_semaphore()

    @pl.loop(1, ROW)
    def _(k):
        pl.semaphore_signal(bar, inc=1, device_id=(g, lax.rem(r + k, ROW)), device_id_type=MESH)

    @pl.loop(1, GX)
    def _(k):
        pl.semaphore_signal(bar, inc=1, device_id=(lax.rem(g + k, GX), r), device_id_type=MESH)

    for i, j in CORNERS:
        where = ((left, right)[i], (below, above)[j])
        pl.semaphore_signal(bar, inc=1, device_id=where, device_id_type=MESH)

    loads = []
    for zh in range(2):
        lanes = pl.ds(128 * zh, 128)
        loads.append(
            pltpu.make_async_copy(
                eddy.at[:, :, :, lanes], f0.at[:, pl.ds(2, 8), zh, pl.ds(8, 32), :], load_sem.at[zh]
            )
        )
    for zh in range(2):
        lanes = pl.ds(128 * zh, 128)
        loads.append(
            pltpu.make_async_copy(
                acoustic.at[:, :, :, lanes],
                ys.at[0, :, pl.ds(3, 16), zh, pl.ds(8, 16), :],
                load_sem.at[2 + zh],
            )
        )
    loads.append(pltpu.make_async_copy(weights, wv, load_sem.at[4]))
    for copy in loads:
        copy.start()

    entry = lax.broadcasted_iota(jnp.int32, (128, 128), 0)
    device = lax.broadcasted_iota(jnp.int32, (128, 128), 1)
    named = jnp.broadcast_to(target[...], (128, 128)).T
    block = jnp.broadcast_to(tblock[...], (128, 128)).T
    hit = (named == device) & (entry < live[0])
    first = jnp.min(jnp.where(hit, entry, 128), axis=0, keepdims=True)
    last = jnp.max(jnp.where(hit, entry, -1), axis=0, keepdims=True)
    id_first = jnp.max(jnp.where(hit & (entry == first), block, -1), axis=0, keepdims=True)
    id_last = jnp.max(jnp.where(hit & (entry == last), block, -1), axis=0, keepdims=True)
    slots[0:1, :] = jnp.where(first < 128, first, 0)
    slots[1:2, :] = jnp.maximum(last, 0)
    lists[me, 0:1, :] = id_first
    lists[me, 1:2, :] = jnp.where(last > first, id_last, -1)
    slot_copy = pltpu.make_async_copy(slots, slots_s, slot_sem)
    slot_copy.start()

    zero = jnp.zeros((8, 128), F32)

    @pl.when(r == 0)
    def _():
        f0[:, :, :, 0:8, :] = jnp.zeros((5, 12, 2, 8, 128), F32)

        @pl.loop(0, 4)
        def _(n):
            ys[n, :, :, :, 0:8, :] = jnp.zeros((4, 22, 2, 8, 128), F32)

    @pl.when(r == ROW - 1)
    def _():
        f0[:, :, :, 40:48, :] = jnp.zeros((5, 12, 2, 8, 128), F32)

        @pl.loop(0, 4)
        def _(n):
            ys[n, :, :, :, 24:32, :] = jnp.zeros((4, 22, 2, 8, 128), F32)

    loads[0].wait()
    loads[1].wait()

    flat0 = f0.reshape(5 * 12 * 2 * FR, 128)

    def flow_row(c, x, zh, row):
        return ((c * 12 + x) * 2 + zh) * FR + row

    for side in range(2):
        for c in range(5):
            for k in range(2):
                for zh in range(2):
                    start = flow_row(c, 2, zh, (8, 38)[side] + k)
                    fsend[side, (c * 2 + k) * 2 + zh] = flat0[pl.ds(start, 8, stride=2 * FR), :]
    for n, (i, j) in enumerate(CORNERS):
        for c in range(5):
            for zh in range(2):
                start = flow_row(c, (2, 9)[i], zh, (8, 39)[j])
                csend[n, 2 * c + zh : 2 * c + zh + 1, :] = flat0[pl.ds(start, 1), :]

    pl.semaphore_wait(bar, ROW - 1 + GX - 1 + 4)

    flow_copies = [
        remote(fsend.at[0], frecv.at[0], fr_s.at[0], fr_r.at[0], (g, below)),
        remote(fsend.at[1], frecv.at[1], fr_s.at[1], fr_r.at[1], (g, above)),
    ]
    for n, (i, j) in enumerate(CORNERS):
        where = ((left, right)[i], (below, above)[j])
        flow_copies.append(remote(csend.at[n], crecv.at[n], fc_s.at[n], fc_r.at[n], where))
    inner = pl.ds(8, 32)
    flow_copies.append(
        remote(
            f0.at[:, pl.ds(2, 2), :, inner, :], f0.at[:, pl.ds(10, 2), :, inner, :],
            fx_s.at[0], fx_r.at[0], (left, r),
        )
    )
    flow_copies.append(
        remote(
            f0.at[:, pl.ds(8, 2), :, inner, :], f0.at[:, pl.ds(0, 2), :, inner, :],
            fx_s.at[1], fx_r.at[1], (right, r),
        )
    )
    for copy in flow_copies:
        copy.start()

    @pl.loop(1, ROW)
    def _(k):
        remote(lists.at[me], lists.at[me], l1_s, l1_r, (g, lax.rem(r + k, ROW))).start()

    def first_step(x, tiles):
        for t in tiles:
            row = 7 + 8 * t

            def emit(zh, new):
                for c in range(5):
                    f1[c, x - 1, zh, pl.ds(row, 8), :] = new[c]

            flow_tile(f0, x, row, lane, emit)

    @pl.loop(3, 9)
    def _(x):
        first_step(x, (1, 2, 3))

    flow_copies[0].wait_recv()
    flow_copies[1].wait_recv()

    def unpack_flow(side):
        for c in range(5):
            for k in range(2):
                for zh in range(2):
                    start = flow_row(c, 2, zh, (40, 6)[side] + k)
                    flat0[pl.ds(start, 8, stride=2 * FR), :] = frecv[side, (c * 2 + k) * 2 + zh]

    @pl.when(r < ROW - 1)
    def _():
        unpack_flow(0)

    @pl.when(r > 0)
    def _():
        unpack_flow(1)

    @pl.loop(3, 9)
    def _(x):
        first_step(x, (0, 4))

    for copy in flow_copies[2:]:
        copy.wait_recv()
    pltpu.make_async_copy(lists.at[pl.ds(0, ROW - 1)], lists.at[pl.ds(0, ROW - 1)], l1_r).wait()
    plane = lists.at[pl.ds(g * ROW, ROW)]

    @pl.loop(1, GX)
    def _(k):
        remote(plane, plane, l2_s, l2_r, (lax.rem(g + k, GX), r)).start()

    for n, (i, j) in enumerate(CORNERS):

        @pl.when(jnp.logical_and((g < GX - 1, g > 0)[i], (r < ROW - 1, r > 0)[j]))
        def _():
            for c in range(5):
                for zh in range(2):
                    start = flow_row(c, (10, 1)[i], zh, (40, 7)[j])
                    flat0[pl.ds(start, 1), :] = crecv[n, 2 * c + zh : 2 * c + zh + 1, :]

    @pl.when(g == 0)
    def _():
        f0[:, 0:2, :, :, :] = jnp.zeros((5, 2, 2, FR, 128), F32)

    @pl.when(g == GX - 1)
    def _():
        f0[:, 10:12, :, :, :] = jnp.zeros((5, 2, 2, FR, 128), F32)

    @pl.loop(0, 4)
    def _(n):
        first_step(n + 1 + 6 * lax.div(n, 2), range(5))

    @pl.when(g == 0)
    def _():
        f1[:, 0, :, :, :] = jnp.zeros((5, 2, FR, 128), F32)

    @pl.when(g == GX - 1)
    def _():
        f1[:, 9, :, :, :] = jnp.zeros((5, 2, FR, 128), F32)

    @pl.when(r == 0)
    def _():
        f1[:, :, :, 7:8, :] = jnp.zeros((5, 10, 2, 1, 128), F32)

    @pl.when(r == ROW - 1)
    def _():
        f1[:, :, :, 40:41, :] = jnp.zeros((5, 10, 2, 1, 128), F32)

    flats = ys.reshape(4 * 4 * 22 * 2 * AR, 128)
    points = pl.ds(8, 16)

    def acoustic_row(n, c, x, zh, row):
        return (((n * 4 + c) * 22 + x) * 2 + zh) * AR + row

    def acoustic_send(n):
        for side in range(2):
            for m, c in enumerate(RADIAL):
                for k in range(3):
                    for zh in range(2):
                        for half in range(2):
                            start = acoustic_row(n, c, 3 + 8 * half, zh, (8, 21)[side] + k)
                            rsend[n, side, (m * 3 + k) * 2 + zh, 8 * half : 8 * half + 8, :] = flats[
                                pl.ds(start, 8, stride=2 * AR), :
                            ]
        copies = [
            remote(rsend.at[n, 0], rrecv.at[n, 0], ar_s.at[n, 0], ar_r.at[n, 0], (g, below)),
            remote(rsend.at[n, 1], rrecv.at[n, 1], ar_s.at[n, 1], ar_r.at[n, 1], (g, above)),
            remote(
                ys.at[n, :, pl.ds(3, 3), :, points, :], ys.at[n, :, pl.ds(19, 3), :, points, :],
                ax_s.at[n, 0], ax_r.at[n, 0], (left, r),
            ),
            remote(
                ys.at[n, :, pl.ds(16, 3), :, points, :], ys.at[n, :, pl.ds(0, 3), :, points, :],
                ax_s.at[n, 1], ax_r.at[n, 1], (right, r),
            ),
        ]
        for copy in copies:
            copy.start()
        return copies

    def acoustic_receive(n, copies):
        for copy in copies:
            copy.wait_recv()

        def unpack(side):
            for m, c in enumerate(RADIAL):
                for k in range(3):
                    for zh in range(2):
                        for half in range(2):
                            start = acoustic_row(n, c, 3 + 8 * half, zh, (24, 5)[side] + k)
                            flats[pl.ds(start, 8, stride=2 * AR), :] = rrecv[
                                n, side, (m * 3 + k) * 2 + zh, 8 * half : 8 * half + 8, :
                            ]

        @pl.when(r < ROW - 1)
        def _():
            unpack(0)

        @pl.when(r > 0)
        def _():
            unpack(1)

        @pl.when(g == 0)
        def _():
            ys[n, :, 0:3, :, 8:24, :] = jnp.zeros((4, 3, 2, 16, 128), F32)

        @pl.when(g == GX - 1)
        def _():
            ys[n, :, 19:22, :, 8:24, :] = jnp.zeros((4, 3, 2, 16, 128), F32)

    loads[2].wait()
    loads[3].wait()
    sent = [acoustic_send(0)]

    @pl.loop(0, 8)
    def _(x):
        for t in range(4):

            def emit(zh, new):
                for c in range(5):
                    f2[c, x, zh, 8 * t : 8 * t + 8, :] = new[c]
                rho = 1.0 + new[0]
                for c, value in enumerate((new[4], rho * new[1], rho * new[2], rho * new[3])):
                    srcs[pl.ds(8 + x * 256 + 64 * t + 4 * zh + c, 8, stride=8), :] = value

            flow_tile(f1, x + 1, 8 + 8 * t, lane, emit)

    out_copies = []
    for zh in range(2):
        lanes = pl.ds(128 * zh, 128)
        out_copies.append(
            pltpu.make_async_copy(f2.at[:, :, zh, :, :], eddy_out.at[:, :, :, lanes], out_sem.at[zh])
        )
        out_copies[-1].start()

    loads[4].wait()

    @pl.loop(0, 8)
    def _(m):
        for u in range(8):
            p = m * 8 + u
            low = srcs[pl.ds(8 + 4 * sblock[2 * p], 8), :]
            high = srcs[pl.ds(4 + 4 * sblock[2 * p + 1], 8), :]
            lhs = jnp.concatenate(
                [jnp.where(sub < 4, low, 0.0), jnp.where(sub < 4, 0.0, high)], axis=1
            ).astype(jnp.bfloat16)
            rhs = jnp.concatenate([wv[2 * p], wv[2 * p + 1]], axis=1)
            contrib[pl.ds(8 + 8 * p, 8), :] = lax.dot_general(
                lhs, rhs, (((1,), (1,)), ((), ())), preferred_element_type=F32
            )

    slot_copy.wait()
    rest = pl.ds(0, DEV - ROW)
    pltpu.make_async_copy(lists.at[rest], lists.at[rest], l2_r).wait()

    def slot_tile(d):
        low = contrib[pl.ds(8 + 4 * jnp.clip(slots_s[0, d], 0, 127), 8), :]
        high = contrib[pl.ds(4 + 4 * jnp.clip(slots_s[1, d], 0, 127), 8), :]
        return jnp.where(sub < 4, low, high)

    @pl.loop(1, DEV)
    def _(k):
        d = lax.rem(me + k, DEV)
        outgoing[d] = slot_tile(d)
        where = (lax.div(d, ROW), lax.rem(d, ROW))
        remote(outgoing.at[d], incoming.at[me], aa_s, aa_r, where).start()

    incoming[me] = slot_tile(me)

    @pl.loop(0, DEV)
    def _(j):
        for k in range(2):
            square[k, pl.ds(j, 1), :] = lists[j, k : k + 1, :]

    for k in range(2):
        turned[k] = square[k].T
    ids = [turned[k, pl.ds(me, 1), :] for k in range(2)]

    @pl.loop(0, 16)
    def _(x):
        place = lax.broadcasted_iota(jnp.int32, (32, 128), 0)
        place = (x * 16 + lax.rem(place, 16)) * 2 + lax.div(place, 16)
        for k in range(2):
            onehot[pl.ds(pl.multiple_of(x * 32, 32), 32), 128 * k : 128 * k + 128] = jnp.where(
                place == ids[k], 1.0, 0.0
            ).astype(jnp.bfloat16)

    acoustic_receive(0, sent[0])

    @pl.loop(0, 16)
    def _(x):
        for t in range(2):
            rate = rate_tile(ys.at[0], x, 8 + 8 * t, lane)
            for zh in range(2):
                for c in range(4):
                    old = ys[0, c, x + 3, zh, 8 + 8 * t : 16 + 8 * t, :]
                    base[c, x, zh, 8 * t : 8 * t + 8, :] = old + (sound_timestep / 4.0) * rate[zh][c]

    others = pl.ds(0, DEV - 1)
    pltpu.make_async_copy(incoming.at[others], incoming.at[others], aa_r).wait()

    flat_in = incoming.reshape((DEV + 1) * 8, 128)
    for pair in range(2):
        value = jnp.concatenate(
            [
                jnp.concatenate(
                    [flat_in[pl.ds(4 * k + 2 * pair + c, DEV, stride=8), :] for k in range(2)], axis=0
                )
                for c in range(2)
            ],
            axis=1,
        )
        high = value.astype(jnp.bfloat16)
        low = (value - high.astype(F32)).astype(jnp.bfloat16)

        @pl.loop(0, 4)
        def _(q):
            rows = onehot[pl.ds(pl.multiple_of(q * 128, 128), 128), :]
            total = jnp.dot(rows, high, preferred_element_type=F32) + jnp.dot(
                rows, low, preferred_element_type=F32
            )
            for c in range(2):
                source[2 * pair + c, pl.ds(pl.multiple_of(q * 128, 128), 128), :] = total[
                    :, 128 * c : 128 * c + 128
                ]

    def source_tile(c, x, zh, t):
        return source[c, pl.ds(pl.multiple_of(x * 32 + zh * 16 + 8 * t, 8), 8), :]

    @pl.loop(0, 16)
    def _(x):
        for t in range(2):
            for zh in range(2):
                for c in range(4):
                    ys[1, c, x + 3, zh, 8 + 8 * t : 16 + 8 * t, :] = (
                        base[c, x, zh, 8 * t : 8 * t + 8, :]
                        + (sound_timestep / 4.0) * source_tile(c, x, zh, t)
                    )

    for n in range(1, 4):
        sent.append(acoustic_send(n))
        acoustic_receive(n, sent[n])
        step = sound_timestep / (4 - n)

        @pl.loop(0, 16)
        def _(x):
            for t in range(2):
                rate = rate_tile(ys.at[n], x, 8 + 8 * t, lane)
                for zh in range(2):
                    for c in range(4):
                        old = ys[0, c, x + 3, zh, 8 + 8 * t : 16 + 8 * t, :]
                        new = old + step * (rate[zh][c] + source_tile(c, x, zh, t))
                        if n < 3:
                            ys[n + 1, c, x + 3, zh, 8 + 8 * t : 16 + 8 * t, :] = new
                        else:
                            final[c, x, zh, 8 * t : 8 * t + 8, :] = new

    for zh in range(2):
        lanes = pl.ds(128 * zh, 128)
        out_copies.append(
            pltpu.make_async_copy(
                final.at[:, :, zh, :, :], acoustic_out.at[:, :, :, lanes], out_sem.at[2 + zh]
            )
        )
        out_copies[-1].start()

    for copy in flow_copies:
        copy.wait_send()
    for copies in sent:
        for copy in copies:
            copy.wait_send()
    pltpu.make_async_copy(lists.at[pl.ds(0, ROW - 1)], lists.at[pl.ds(0, ROW - 1)], l1_s).wait()
    pltpu.make_async_copy(lists.at[rest], lists.at[rest], l2_s).wait()
    pltpu.make_async_copy(outgoing.at[others], outgoing.at[others], aa_s).wait()
    for copy in out_copies:
        copy.wait()


def body(eddy, acoustic, weights, source_block, target_device, target_block, live_count):
    vmem, dma = pltpu.VMEM, pltpu.SemaphoreType.DMA
    anywhere = pl.BlockSpec(memory_space=pl.ANY)
    in_vmem = pl.BlockSpec(memory_space=pltpu.VMEM)
    in_smem = pl.BlockSpec(memory_space=pltpu.SMEM)
    return pl.pallas_call(
        kernel,
        out_shape=(
            jax.ShapeDtypeStruct(eddy.shape, F32),
            jax.ShapeDtypeStruct(acoustic.shape, F32),
        ),
        in_specs=[anywhere, anywhere, anywhere, in_vmem, in_vmem, in_smem, in_smem],
        out_specs=(anywhere, anywhere),
        scratch_shapes=[
            vmem((5, 12, 2, FR, 128), F32),
            vmem((5, 10, 2, FR, 128), F32),
            vmem((5, 8, 2, 32, 128), F32),
            vmem((2048 + 16, 128), F32),
            vmem((128, 128, 128), jnp.bfloat16),
            vmem((512 + 16, 128), F32),
            vmem((DEV, 8, 128), F32),
            vmem((DEV + 1, 8, 128), F32),
            vmem((4, 4, 22, 2, AR, 128), F32),
            vmem((4, 2, 12, 16, 128), F32),
            vmem((4, 2, 12, 16, 128), F32),
            vmem((2, 20, 8, 128), F32),
            vmem((2, 20, 8, 128), F32),
            vmem((4, 16, 128), F32),
            vmem((4, 16, 128), F32),
            vmem((DEV, 2, 128), jnp.int32),
            vmem((2, DEV, 128), jnp.int32),
            vmem((2, DEV, 128), jnp.int32),
            vmem((2, 128), jnp.int32),
            pltpu.SMEM((2, 128), jnp.int32),
            vmem((512, 256), jnp.bfloat16),
            vmem((4, 512, 128), F32),
            vmem((4, 16, 2, 16, 128), F32),
            vmem((4, 16, 2, 16, 128), F32),
            dma((5,)), dma,
            dma((2,)), dma((2,)), dma((2,)), dma((2,)), dma((4,)), dma((4,)),
            dma, dma, dma, dma, dma, dma,
            dma((4, 2)), dma((4, 2)), dma((4, 2)), dma((4, 2)), dma((4,)),
        ],
        compiler_params=pltpu.CompilerParams(
            collective_id=0, has_side_effects=True, vmem_limit_bytes=52 * 1024 * 1024
        ),
        name="jet_step",
    )(
        eddy,
        acoustic,
        weights.reshape(128, 128, 128),
        target_device.reshape(1, 128),
        target_block.reshape(1, 128),
        source_block.reshape(128),
        live_count.reshape(1),
    )


def solution(mesh):
    placed = (
        P(None, "gx", "row", None),
        P(None, "gx", "row", None),
        P("gx", "row", None, None, None),
        P("gx", "row", None),
        P("gx", "row", None, None),
        P("gx", "row", None),
        P("gx", "row"),
    )
    return jax.shard_map(
        body,
        mesh=mesh,
        in_specs=placed,
        out_specs=(P(None, "gx", "row", None), P(None, "gx", "row", None)),
        check_vma=False,
    )
```

profile of v0, /device:TPU:0, one launch (start us, length us, event | category | flops | bytes accessed | tf_op | source)
XLA Modules:
  0.0 63.0 jit_solution(3366535999726087435)
XLA Ops:
  1.3 0.0 copy-start
  1.3 0.6 %copy-done = s32[1,1,128,1]{2,3,1,0:T(1,128)S(1)} copy-done((s32[1,1,128,1]{2,3,1,0:T(1,128)S(1)}, s32[1,1,128,1]{2,3,1,0:T(1,128)}, u32[]{:S(2)}) %copy-start) | copy-done | bytes 536
  1.9 0.0 copy-start.1
  1.9 0.7 %copy-done.1 = s32[1,1,128]{2,1,0:T(1,128)S(1)} copy-done((s32[1,1,128]{2,1,0:T(1,128)S(1)}, s32[1,1,128]{2,1,0:T(1,128)}, u32[]{:S(2)}) %copy-start.1) | copy-done | bytes 536
  2.6 0.0 copy-start.2
  2.6 0.7 %copy-done.2 = s32[1,1,128]{2,1,0:T(1,128)S(1)} copy-done((s32[1,1,128]{2,1,0:T(1,128)S(1)}, s32[1,1,128]{2,1,0:T(1,128)}, u32[]{:S(2)}) %copy-start.2) | copy-done | bytes 536
  3.2 56.3 %jet_step.1 = (f32[5,8,32,256]{3,2,1,0:T(8,128)}, f32[4,16,16,256]{3,2,1,0:T(8,128)S(1)}) custom-call(f32[5,8,32,256]{3,2,1,0:T(8,128)} %eddy.1, f32[4,16,16,256]{3,2,1,0:T(8,128)} %acoustic.1, bf16[128,128,128]{2,1,0:T(8,128)(2,1)} %bitcast.9, s32[1,128]{1,0:T(1,128)S(1)} %bitcast.6, s32[1,128]{1,0:T(1,128)S(1)} %bitcast.7, s32[128]{0:T(128)S(1)} %bitcast.8, ...), custom_call_target="tpu_custom_call" | custom-call | tf_op jit(solution)/shard_map/jet_step/pallas_call | solution.py:569
  59.5 2.5 %copy.12 = f32[5,8,32,256]{3,2,1,0:T(8,128)} copy(f32[5,8,32,256]{3,2,1,0:T(8,128)} %get-tuple-element.4) | data formatting | bytes 2621440
  62.0 1.0 %copy.13 = f32[4,16,16,256]{3,2,1,0:T(8,128)} copy(f32[4,16,16,256]{3,2,1,0:T(8,128)S(1)} %get-tuple-element.5) | data formatting | bytes 2097152
Async XLA Ops:
  1.3 0.7 %copy-start = (s32[1,1,128,1]{2,3,1,0:T(1,128)S(1)}, s32[1,1,128,1]{2,3,1,0:T(1,128)}, u32[]{:S(2)}) copy-start(s32[1,1,128,1]{2,3,1,0:T(1,128)} %param.11) | copy-start | bytes 1540
  1.9 0.7 %copy-start.1 = (s32[1,1,128]{2,1,0:T(1,128)S(1)}, s32[1,1,128]{2,1,0:T(1,128)}, u32[]{:S(2)}) copy-start(s32[1,1,128]{2,1,0:T(1,128)} %param.12) | copy-start | bytes 1540
  2.6 0.7 %copy-start.2 = (s32[1,1,128]{2,1,0:T(1,128)S(1)}, s32[1,1,128]{2,1,0:T(1,128)}, u32[]{:S(2)}) copy-start(s32[1,1,128]{2,1,0:T(1,128)} %param.10) | copy-start | bytes 1540
where the time goes:
time: 63.2 us; the launch traced here: 63 us
  Pallas kernels  56.3 us (89%)
  local copies, waits for them, and re-layouts  5.45 us (9%)
  between operations  1.3 us (2%)
    pallas_call x1, Pallas kernels, body(): pl.pallas_call(kernel, out_shape=(jax.ShapeDtypeStruct(eddy.shape, F32),...  56.3 us
    unnamed x8, local copies, waits for them, and re-layouts  5.45 us

commit v1 on v0

v1 whole, which is shorter than its diff:
```python
import functools

import jax
import jax.numpy as jnp
from jax import lax
from jax.experimental import pallas as pl
from jax.experimental.pallas import tpu as pltpu
from jax.sharding import PartitionSpec as P

MESH = pl.DeviceIdType.MESH
F32 = jnp.float32

gamma_gas = 1.4
sound_timestep = 0.5
mean_mach = 0.3
stencil = (0.75, -0.15, 1.0 / 60.0)

GX = 8
ROW = 16
DEV = GX * ROW
FR = 48
AR = 32
CORNERS = ((0, 0), (0, 1), (1, 0), (1, 1))
RADIAL = (0, 2)


def shifted(low, high, lane, step):
    if step > 0:
        a, b = pltpu.roll(low, 128 - step, 1), pltpu.roll(high, 128 - step, 1)
        keep = lane < 128 - step
    else:
        a, b = pltpu.roll(low, -step, 1), pltpu.roll(high, -step, 1)
        keep = lane >= -step
    return jnp.where(keep, a, b), jnp.where(keep, b, a)


def flow_tile(src, x, row, lane, emit):
    rows = pl.ds(row, 8)
    center = [[src[c, x, zh, rows, :] for zh in range(2)] for c in range(5)]
    upper = [shifted(center[c][0], center[c][1], lane, 1) for c in range(5)]
    lower = [shifted(center[c][0], center[c][1], lane, -1) for c in range(5)]
    for zh in range(2):
        dx, dr, dz, lap = [], [], [], []
        for c in range(5):
            xp, xm = src[c, x + 1, zh, rows, :], src[c, x - 1, zh, rows, :]
            rp, rm = src[c, x, zh, pl.ds(row + 1, 8), :], src[c, x, zh, pl.ds(row - 1, 8), :]
            zp, zm = upper[c][zh], lower[c][zh]
            dx.append(xp - xm)
            dr.append(rp - rm)
            dz.append(zp - zm)
            lap.append(((xp + xm) + (rp + rm)) + ((zp + zm) - 6.0 * center[c][zh]))
        q = [center[c][zh] for c in range(5)]
        div = dx[1] + dr[2] + dz[3]
        rho = 1.0 + q[0]
        inv = 1.0 / rho
        force = (
            rho * div,
            dx[4] * inv,
            dr[4] * inv,
            dz[4] * inv,
            (gamma_gas * q[4] + 1.0) * div,
        )
        new = []
        for c in range(5):
            adv = q[1] * dx[c] + q[2] * dr[c] + q[3] * dz[c]
            new.append(q[c] + 0.1 * (lap[c] - adv - force[c]))
        emit(zh, new)


def rate_tile(src, x, row, lane):
    rows = pl.ds(row, 8)

    def grad_x(c, zh):
        total = None
        for k in range(3):
            part = stencil[k] * (src[c, x + 4 + k, zh, rows, :] - src[c, x + 2 - k, zh, rows, :])
            total = part if total is None else total + part
        return total

    def grad_r(c, zh):
        total = None
        for k in range(3):
            part = stencil[k] * (
                src[c, x + 3, zh, pl.ds(row + k + 1, 8), :]
                - src[c, x + 3, zh, pl.ds(row - k - 1, 8), :]
            )
            total = part if total is None else total + part
        return total

    def grad_z(c):
        low, high = src[c, x + 3, 0, rows, :], src[c, x + 3, 1, rows, :]
        total = None
        for k in range(3):
            up = shifted(low, high, lane, k + 1)
            down = shifted(low, high, lane, -k - 1)
            part = [stencil[k] * (up[zh] - down[zh]) for zh in range(2)]
            total = part if total is None else [total[zh] + part[zh] for zh in range(2)]
        return total

    zp, zw = grad_z(0), grad_z(3)
    out = []
    for zh in range(2):
        xp, xu, xv, xw = (grad_x(c, zh) for c in range(4))
        out.append(
            (
                -(mean_mach * xp + xu + grad_r(2, zh) + zw[zh]),
                -(mean_mach * xu + xp),
                -(mean_mach * xv + grad_r(0, zh)),
                -(mean_mach * xw + zp[zh]),
            )
        )
    return out


def kernel(
    eddy, acoustic, weights, numbers, eddy_out, final,
    f0, f1, f2, srcs, wv, contrib, outgoing, incoming, ys, rsend, rrecv, xrecv, fsend, frecv, csend, crecv,
    numbers_s, lists, square, turned, slots, slots_s, onehot, source,
    load_sem, small_sem, slot_sem, fx_s, fx_r, fr_s, fr_r, fc_s, fc_r, l1_s, l1_r, l2_s, l2_r, aa_s, aa_r,
    ax_s, ax_r, ar_s, ar_r, plane_in, all_in, out_sem,
):
    g, r = lax.axis_index("gx"), lax.axis_index("row")
    me = g * ROW + r
    left, right = lax.rem(g + GX - 1, GX), lax.rem(g + 1, GX)
    below, above = lax.rem(r + ROW - 1, ROW), lax.rem(r + 1, ROW)
    ry, rz = lax.div(r, 4), lax.rem(r, 4)
    lane = lax.broadcasted_iota(jnp.int32, (8, 128), 1)
    sub = lax.broadcasted_iota(jnp.int32, (8, 128), 0)
    zero = jnp.zeros((8, 128), F32)

    def remote(src, dst, send, recv, where):
        return pltpu.make_async_remote_copy(
            src_ref=src, dst_ref=dst, send_sem=send, recv_sem=recv, device_id=where, device_id_type=MESH
        )

    def signal(sem, where):
        pl.semaphore_signal(sem, inc=1, device_id=where, device_id_type=MESH)

    def y_line(k):
        return g, lax.rem(ry + k, 4) * 4 + rz

    def x_line(k):
        return lax.rem(g + k, GX), r

    small = pltpu.make_async_copy(numbers, numbers_s, small_sem)
    small.start()

    bar = pltpu.get_barrier_semaphore()
    for i, j in CORNERS:
        signal(bar, ((left, right)[i], (below, above)[j]))
    signal(bar, (g, below))
    signal(bar, (g, above))
    for k in range(1, 4):
        signal(bar, y_line(k))
        signal(bar, (g, ry * 4 + lax.rem(rz + k, 4)))
    for k in range(1, GX):
        signal(bar, x_line(k))

    loads = []
    for zh in range(2):
        lanes = pl.ds(128 * zh, 128)
        loads.append(
            pltpu.make_async_copy(
                eddy.at[:, :, :, lanes], f0.at[:, pl.ds(2, 8), zh, pl.ds(8, 32), :], load_sem.at[zh]
            )
        )
    for zh in range(2):
        lanes = pl.ds(128 * zh, 128)
        loads.append(
            pltpu.make_async_copy(
                acoustic.at[:, :, :, lanes],
                ys.at[0, :, pl.ds(3, 16), zh, pl.ds(8, 16), :],
                load_sem.at[2 + zh],
            )
        )
    loads.append(pltpu.make_async_copy(weights, wv, load_sem.at[4]))
    for copy in loads:
        copy.start()

    @pl.loop(0, 4)
    def _(n):
        @pl.loop(0, 3)
        def _(x):
            for c in range(4):
                for zh in range(2):
                    for line in (x, x + 19):
                        for t in (8, 16):
                            ys[n, c, line, zh, t : t + 8, :] = zero

        @pl.loop(3, 19)
        def _(x):
            for c in RADIAL:
                for zh in range(2):
                    for t in (0, 24):
                        ys[n, c, x, zh, t : t + 8, :] = zero

    @pl.when(r == 0)
    def _():
        f0[:, :, :, 0:8, :] = jnp.zeros((5, 12, 2, 8, 128), F32)

    @pl.when(r == ROW - 1)
    def _():
        f0[:, :, :, 40:48, :] = jnp.zeros((5, 12, 2, 8, 128), F32)

    entry = lax.broadcasted_iota(jnp.int32, (128, 128), 0)
    device = lax.broadcasted_iota(jnp.int32, (128, 128), 1)
    named = jnp.broadcast_to(numbers[0:1, :], (128, 128)).T
    block = jnp.broadcast_to(numbers[1:2, :], (128, 128)).T
    hit = (named == device) & (entry < numbers[3:4, :])
    first = jnp.min(jnp.where(hit, entry, 128), axis=0, keepdims=True)
    last = jnp.max(jnp.where(hit, entry, -1), axis=0, keepdims=True)
    id_first = jnp.max(jnp.where(hit & (entry == first), block, -1), axis=0, keepdims=True)
    id_last = jnp.max(jnp.where(hit & (entry == last), block, -1), axis=0, keepdims=True)
    slots[0:1, :] = jnp.where(first < 128, first, 0)
    slots[1:2, :] = jnp.maximum(last, 0)
    lists[me, 0:1, :] = id_first
    lists[me, 1:2, :] = jnp.where(last > first, id_last, -1)
    slot_copy = pltpu.make_async_copy(slots, slots_s, slot_sem)
    slot_copy.start()

    loads[0].wait()
    loads[1].wait()

    flat0 = f0.reshape(5 * 12 * 2 * FR, 128)

    def flow_row(c, x, zh, row):
        return ((c * 12 + x) * 2 + zh) * FR + row

    for side in range(2):
        for c in range(5):
            for k in range(2):
                for zh in range(2):
                    start = flow_row(c, 2, zh, (8, 38)[side] + k)
                    fsend[side, (c * 2 + k) * 2 + zh] = flat0[pl.ds(start, 8, stride=2 * FR), :]
    for n, (i, j) in enumerate(CORNERS):
        for c in range(5):
            for zh in range(2):
                start = flow_row(c, (2, 9)[i], zh, (8, 39)[j])
                csend[n, 2 * c + zh : 2 * c + zh + 1, :] = flat0[pl.ds(start, 1), :]

    inner = pl.ds(8, 32)
    flow_copies = [
        remote(fsend.at[0], frecv.at[0], fr_s.at[0], fr_r.at[0], (g, below)),
        remote(fsend.at[1], frecv.at[1], fr_s.at[1], fr_r.at[1], (g, above)),
        remote(
            f0.at[:, pl.ds(2, 2), :, inner, :], f0.at[:, pl.ds(10, 2), :, inner, :],
            fx_s.at[0], fx_r.at[0], (left, r),
        ),
        remote(
            f0.at[:, pl.ds(8, 2), :, inner, :], f0.at[:, pl.ds(0, 2), :, inner, :],
            fx_s.at[1], fx_r.at[1], (right, r),
        ),
    ]
    for n, (i, j) in enumerate(CORNERS):
        where = ((left, right)[i], (below, above)[j])
        flow_copies.append(remote(csend.at[n], crecv.at[n], fc_s.at[n], fc_r.at[n], where))

    pl.semaphore_wait(bar, 4 + 2 + 6 + GX - 1)
    for copy in flow_copies:
        copy.start()
    for k in range(1, 4):
        signal(plane_in, y_line(k))

    def first_step(x, tiles):
        for t in tiles:
            row = 7 + 8 * t

            def emit(zh, new):
                for c in range(5):
                    f1[c, x - 1, zh, pl.ds(row, 8), :] = new[c]

            flow_tile(f0, x, row, lane, emit)

    @pl.loop(3, 9, unroll=2)
    def _(x):
        first_step(x, (1, 2, 3))

    pl.semaphore_wait(plane_in, 3)
    for k in range(1, GX):
        signal(all_in, x_line(k))

    @pl.loop(1, ROW)
    def _(k):
        remote(lists.at[me], lists.at[me], l1_s, l1_r, (g, lax.rem(r + k, ROW))).start()

    flow_copies[0].wait_recv()
    flow_copies[1].wait_recv()

    def unpack_flow(side):
        for c in range(5):
            for k in range(2):
                for zh in range(2):
                    start = flow_row(c, 2, zh, (40, 6)[side] + k)
                    flat0[pl.ds(start, 8, stride=2 * FR), :] = frecv[side, (c * 2 + k) * 2 + zh]

    @pl.when(r < ROW - 1)
    def _():
        unpack_flow(0)

    @pl.when(r > 0)
    def _():
        unpack_flow(1)

    @pl.loop(3, 9, unroll=2)
    def _(x):
        first_step(x, (0, 4))

    for copy in flow_copies[2:]:
        copy.wait_recv()

    flats = ys.reshape(4 * 4 * 22 * 2 * AR, 128)
    points = pl.ds(8, 16)

    def acoustic_row(n, c, x, zh, row):
        return (((n * 4 + c) * 22 + x) * 2 + zh) * AR + row

    def acoustic_pack(n):
        for side in range(2):
            for m, c in enumerate(RADIAL):
                for k in range(3):
                    for zh in range(2):
                        for half in range(2):
                            start = acoustic_row(n, c, 3 + 8 * half, zh, (8, 21)[side] + k)
                            rsend[n, side, (m * 3 + k) * 2 + zh, 8 * half : 8 * half + 8, :] = flats[
                                pl.ds(start, 8, stride=2 * AR), :
                            ]

    def acoustic_send(n):
        copies = [
            remote(rsend.at[n, 0], rrecv.at[n, 0], ar_s.at[n, 0], ar_r.at[n, 0], (g, below)),
            remote(rsend.at[n, 1], rrecv.at[n, 1], ar_s.at[n, 1], ar_r.at[n, 1], (g, above)),
            remote(
                ys.at[n, :, pl.ds(3, 3), :, points, :], xrecv.at[n, 0],
                ax_s.at[n, 0], ax_r.at[n, 0], (left, r),
            ),
            remote(
                ys.at[n, :, pl.ds(16, 3), :, points, :], xrecv.at[n, 1],
                ax_s.at[n, 1], ax_r.at[n, 1], (right, r),
            ),
        ]
        for copy in copies:
            copy.start()
        return copies

    loads[2].wait()
    loads[3].wait()
    acoustic_pack(0)
    sent = [acoustic_send(0)]

    for n, (i, j) in enumerate(CORNERS):

        @pl.when(jnp.logical_and((g < GX - 1, g > 0)[i], (r < ROW - 1, r > 0)[j]))
        def _():
            for c in range(5):
                for zh in range(2):
                    start = flow_row(c, (10, 1)[i], zh, (40, 7)[j])
                    flat0[pl.ds(start, 1), :] = crecv[n, 2 * c + zh : 2 * c + zh + 1, :]

    @pl.when(g == 0)
    def _():
        f0[:, 0:2, :, :, :] = jnp.zeros((5, 2, 2, FR, 128), F32)

    @pl.when(g == GX - 1)
    def _():
        f0[:, 10:12, :, :, :] = jnp.zeros((5, 2, 2, FR, 128), F32)

    @pl.loop(0, 4, unroll=2)
    def _(n):
        first_step(n + 1 + 6 * lax.div(n, 2), range(5))

    @pl.when(g == 0)
    def _():
        f1[:, 0, :, :, :] = jnp.zeros((5, 2, FR, 128), F32)

    @pl.when(g == GX - 1)
    def _():
        f1[:, 9, :, :, :] = jnp.zeros((5, 2, FR, 128), F32)

    @pl.when(r == 0)
    def _():
        f1[:, :, :, 7:8, :] = jnp.zeros((5, 10, 2, 1, 128), F32)

    @pl.when(r == ROW - 1)
    def _():
        f1[:, :, :, 40:41, :] = jnp.zeros((5, 10, 2, 1, 128), F32)

    @pl.loop(0, 8, unroll=2)
    def _(x):
        for t in range(4):

            def emit(zh, new):
                for c in range(5):
                    f2[c, x, 8 * t : 8 * t + 8, 128 * zh : 128 * zh + 128] = new[c]
                rho = 1.0 + new[0]
                for c, value in enumerate((new[4], rho * new[1], rho * new[2], rho * new[3])):
                    srcs[pl.ds(8 + x * 256 + 64 * t + 4 * zh + c, 8, stride=8), :] = value

            flow_tile(f1, x + 1, 8 + 8 * t, lane, emit)

    flow_out = pltpu.make_async_copy(f2, eddy_out, out_sem)
    flow_out.start()
    pltpu.make_async_copy(lists.at[pl.ds(0, ROW - 1)], lists.at[pl.ds(0, ROW - 1)], l1_r).wait()
    pl.semaphore_wait(all_in, GX - 1)
    plane = lists.at[pl.ds(g * ROW, ROW)]

    @pl.loop(1, GX)
    def _(k):
        remote(plane, plane, l2_s, l2_r, x_line(k)).start()

    loads[4].wait()
    small.wait()

    @pl.loop(0, 8)
    def _(m):
        for u in range(8):
            p = m * 8 + u
            low = srcs[pl.ds(8 + 4 * numbers_s[2, 2 * p], 8), :]
            high = srcs[pl.ds(4 + 4 * numbers_s[2, 2 * p + 1], 8), :]
            lhs = jnp.concatenate(
                [jnp.where(sub < 4, low, 0.0), jnp.where(sub < 4, 0.0, high)], axis=1
            ).astype(jnp.bfloat16)
            rhs = jnp.concatenate([wv[2 * p], wv[2 * p + 1]], axis=1)
            contrib[pl.ds(8 + 8 * p, 8), :] = lax.dot_general(
                lhs, rhs, (((1,), (1,)), ((), ())), preferred_element_type=F32
            )

    slot_copy.wait()

    def slot_tile(d):
        low = contrib[pl.ds(8 + 4 * jnp.clip(slots_s[0, d], 0, 127), 8), :]
        high = contrib[pl.ds(4 + 4 * jnp.clip(slots_s[1, d], 0, 127), 8), :]
        return jnp.where(sub < 4, low, high)

    @pl.loop(1, DEV)
    def _(k):
        d = lax.rem(me + k, DEV)
        outgoing[d] = slot_tile(d)
        where = (lax.div(d, ROW), lax.rem(d, ROW))
        remote(outgoing.at[d], incoming.at[me], aa_s, aa_r, where).start()

    incoming[me] = slot_tile(me)

    def source_tile(c, x, zh, t):
        return source[c, pl.ds(pl.multiple_of(x * 32 + zh * 16 + 8 * t, 8), 8), :]

    def stage_bulk(n, step):
        @pl.loop(0, 16, unroll=4)
        def _(x):
            for t in range(2):
                rate = rate_tile(ys.at[n], x, 8 + 8 * t, lane)
                for zh in range(2):
                    for c in range(4):
                        old = ys[0, c, x + 3, zh, 8 + 8 * t : 16 + 8 * t, :]
                        change = rate[zh][c]
                        if n > 0:
                            change = change + source_tile(c, x, zh, t)
                        new = old + step * change
                        if n < 3:
                            ys[n + 1, c, x + 3, zh, 8 + 8 * t : 16 + 8 * t, :] = new
                        else:
                            final[c, x, 8 * t : 8 * t + 8, 128 * zh : 128 * zh + 128] = new

    def halo_share(lines, ell, upper):
        total = None
        for k in range(ell + 1, 4):
            part = stencil[k - 1] * (lines[k - ell - 1] if upper else lines[ell - k + 3])
            total = part if total is None else total + part
        return total if upper else -total

    def fix_x(n, step, side):
        for zh in range(2):
            for t in range(2):
                rows = pl.ds(8 * t, 8)
                halo = [[xrecv[n, side, c, k, zh, rows, :] for k in range(3)] for c in range(4)]
                for ell in range(3):
                    x = ell if side else 15 - ell
                    gp, gu, gv, gw = (halo_share(halo[c], ell, side == 0) for c in range(4))
                    changes = (mean_mach * gp + gu, mean_mach * gu + gp, mean_mach * gv, mean_mach * gw)
                    for c in range(4):
                        if n < 3:
                            at = (n + 1, c, x + 3, zh, pl.ds(8 + 8 * t, 8), slice(None))
                            ys[at] = ys[at] - step * changes[c]
                        else:
                            at = (c, x, rows, pl.ds(128 * zh, 128))
                            final[at] = final[at] - step * changes[c]

    def clear_ends(n):
        @pl.when(r == ROW - 1)
        def _():
            rrecv[n, 0] = jnp.zeros((12, 16, 128), F32)

        @pl.when(r == 0)
        def _():
            rrecv[n, 1] = jnp.zeros((12, 16, 128), F32)

    def fix_r(n, step):
        for side in range(2):
            for zh in range(2):
                for half in range(2):
                    eight = pl.ds(8 * half, 8)
                    halo = [
                        [rrecv[n, side, (m * 3 + k) * 2 + zh, eight, :] for k in range(3)] for m in range(2)
                    ]
                    for ell in range(3):
                        row = ell if side else 15 - ell
                        for m, c in enumerate(RADIAL):
                            change = step * halo_share(halo[1 - m], ell, side == 0)
                            start = acoustic_row(n + 1, c, 3 + 8 * half, zh, 8 + row)
                            at = pl.ds(start, 8, stride=2 * AR)
                            new = flats[at, :] - change
                            flats[at, :] = new
                            if n > 0:
                                k = ell if side else 2 - ell
                                rsend[n + 1, 1 - side, (m * 3 + k) * 2 + zh, eight, :] = new

    def fix_r_last(n, step):
        for side in range(2):
            for m, c in enumerate(RADIAL):
                for k in range(3):
                    for zh in range(2):
                        for half in range(2):
                            start = acoustic_row(n, c, 3 + 8 * half, zh, (24, 5)[side] + k)
                            flats[pl.ds(start, 8, stride=2 * AR), :] = rrecv[
                                n, side, (m * 3 + k) * 2 + zh, 8 * half : 8 * half + 8, :
                            ]

        @pl.loop(0, 16, unroll=4)
        def _(x):
            for side in range(2):
                for zh in range(2):
                    for m, c in enumerate(RADIAL):
                        other = RADIAL[1 - m]
                        total = None
                        for k in range(1, 4):
                            if side:
                                part = jnp.where(sub < k, ys[n, other, x + 3, zh, pl.ds(8 - k, 8), :], 0.0)
                                part = (-step * stencil[k - 1]) * part
                            else:
                                part = jnp.where(sub >= 8 - k, ys[n, other, x + 3, zh, pl.ds(16 + k, 8), :], 0.0)
                                part = (step * stencil[k - 1]) * part
                            total = part if total is None else total + part
                        at = (c, x, pl.ds(0 if side else 8, 8), pl.ds(128 * zh, 128))
                        final[at] = final[at] - total

    def stage_fix(n, step):
        sent[n][2].wait_recv()
        sent[n][3].wait_recv()

        @pl.when(g < GX - 1)
        def _():
            fix_x(n, step, 0)

        @pl.when(g > 0)
        def _():
            fix_x(n, step, 1)

        sent[n][0].wait_recv()
        sent[n][1].wait_recv()
        clear_ends(n)
        if n < 3:
            fix_r(n, step)
        else:
            fix_r_last(n, step)

    stage_bulk(0, sound_timestep / 4.0)
    stage_fix(0, sound_timestep / 4.0)

    rest = pl.ds(0, DEV - ROW)
    pltpu.make_async_copy(lists.at[rest], lists.at[rest], l2_r).wait()

    @pl.loop(0, DEV, unroll=8)
    def _(j):
        for k in range(2):
            square[k, pl.ds(j, 1), :] = lists[j, k : k + 1, :]

    for k in range(2):
        turned[k] = square[k].T
    ids = [turned[k, pl.ds(me, 1), :] for k in range(2)]

    @pl.loop(0, 16)
    def _(x):
        place = lax.broadcasted_iota(jnp.int32, (32, 128), 0)
        place = (x * 16 + lax.rem(place, 16)) * 2 + lax.div(place, 16)
        for k in range(2):
            onehot[pl.ds(pl.multiple_of(x * 32, 32), 32), 128 * k : 128 * k + 128] = jnp.where(
                place == ids[k], 1.0, 0.0
            ).astype(jnp.bfloat16)

    others = pl.ds(0, DEV - 1)
    pltpu.make_async_copy(incoming.at[others], incoming.at[others], aa_r).wait()

    flat_in = incoming.reshape((DEV + 1) * 8, 128)
    for pair in range(2):
        value = jnp.concatenate(
            [
                jnp.concatenate(
                    [flat_in[pl.ds(4 * k + 2 * pair + c, DEV, stride=8), :] for k in range(2)], axis=0
                )
                for c in range(2)
            ],
            axis=1,
        )
        high = value.astype(jnp.bfloat16)
        low = (value - high.astype(F32)).astype(jnp.bfloat16)

        @pl.loop(0, 4)
        def _(q):
            rows = onehot[pl.ds(pl.multiple_of(q * 128, 128), 128), :]
            total = jnp.dot(rows, high, preferred_element_type=F32) + jnp.dot(
                rows, low, preferred_element_type=F32
            )
            for c in range(2):
                part = total[:, 128 * c : 128 * c + 128]
                source[2 * pair + c, pl.ds(pl.multiple_of(q * 128, 128), 128), :] = part
                for i in range(4):
                    for zh in range(2):
                        at = (1, 2 * pair + c, q * 4 + i + 3, zh, points, slice(None))
                        piece = part[32 * i + 16 * zh : 32 * i + 16 * zh + 16, :]
                        ys[at] = ys[at] + (sound_timestep / 4.0) * piece

    acoustic_pack(1)
    for n in range(1, 4):
        sent.append(acoustic_send(n))
        stage_bulk(n, sound_timestep / (4 - n))
        stage_fix(n, sound_timestep / (4 - n))

    for copy in flow_copies:
        copy.wait_send()
    for copies in sent:
        for copy in copies:
            copy.wait_send()
    pltpu.make_async_copy(lists.at[pl.ds(0, ROW - 1)], lists.at[pl.ds(0, ROW - 1)], l1_s).wait()
    pltpu.make_async_copy(lists.at[rest], lists.at[rest], l2_s).wait()
    pltpu.make_async_copy(outgoing.at[others], outgoing.at[others], aa_s).wait()
    flow_out.wait()


def body(eddy, acoustic, weights, source_block, target_device, target_block, live_count):
    vmem, dma, regular = pltpu.VMEM, pltpu.SemaphoreType.DMA, pltpu.SemaphoreType.REGULAR
    anywhere = pl.BlockSpec(memory_space=pl.ANY)
    in_vmem = pl.BlockSpec(memory_space=pltpu.VMEM)
    numbers = jnp.concatenate(
        [
            target_device.reshape(1, 128),
            target_block.reshape(1, 128),
            source_block.reshape(1, 128),
            jnp.broadcast_to(live_count, (1, 128)),
        ]
    )
    return pl.pallas_call(
        kernel,
        out_shape=(
            jax.ShapeDtypeStruct(eddy.shape, F32),
            jax.ShapeDtypeStruct(acoustic.shape, F32),
        ),
        in_specs=[anywhere] * 3 + [in_vmem],
        out_specs=(anywhere, in_vmem),
        scratch_shapes=[
            vmem((5, 12, 2, FR, 128), F32),
            vmem((5, 10, 2, FR, 128), F32),
            vmem((5, 8, 32, 256), F32),
            vmem((2048 + 16, 128), F32),
            vmem((128, 128, 128), jnp.bfloat16),
            vmem((512 + 16, 128), F32),
            vmem((DEV, 8, 128), F32),
            vmem((DEV + 1, 8, 128), F32),
            vmem((4, 4, 22, 2, AR, 128), F32),
            vmem((4, 2, 12, 16, 128), F32),
            vmem((4, 2, 12, 16, 128), F32),
            vmem((4, 2, 4, 3, 2, 16, 128), F32),
            vmem((2, 20, 8, 128), F32),
            vmem((2, 20, 8, 128), F32),
            vmem((4, 16, 128), F32),
            vmem((4, 16, 128), F32),
            pltpu.SMEM((4, 128), jnp.int32),
            vmem((DEV, 2, 128), jnp.int32),
            vmem((2, DEV, 128), jnp.int32),
            vmem((2, DEV, 128), jnp.int32),
            vmem((2, 128), jnp.int32),
            pltpu.SMEM((2, 128), jnp.int32),
            vmem((512, 256), jnp.bfloat16),
            vmem((4, 512, 128), F32),
            dma((5,)), dma, dma,
            dma((2,)), dma((2,)), dma((2,)), dma((2,)), dma((4,)), dma((4,)),
            dma, dma, dma, dma, dma, dma,
            dma((4, 2)), dma((4, 2)), dma((4, 2)), dma((4, 2)), regular, regular, dma,
        ],
        compiler_params=pltpu.CompilerParams(
            collective_id=0, has_side_effects=True, vmem_limit_bytes=52 * 1024 * 1024
        ),
        name="jet_step",
    )(
        eddy,
        acoustic,
        weights.reshape(128, 128, 128),
        numbers,
    )


def solution(mesh):
    placed = (
        P(None, "gx", "row", None),
        P(None, "gx", "row", None),
        P("gx", "row", None, None, None),
        P("gx", "row", None),
        P("gx", "row", None, None),
        P("gx", "row", None),
        P("gx", "row"),
    )
    return jax.shard_map(
        body,
        mesh=mesh,
        in_specs=placed,
        out_specs=(P(None, "gx", "row", None), P(None, "gx", "row", None)),
        check_vma=False,
    )
```

time: 63.2 us -> 56 us (0.89)
  Pallas kernels: 56.3 us -> 50.3 us
  local copies, waits for them, and re-layouts: 5.45 us -> 3.56 us
  other arithmetic: 0 us -> 0.76 us
    pallas_call x1, Pallas kernels: 56.3 us -> 50.3 us  [body(): pl.pallas_call(kernel, out_shape=(jax.ShapeDtypeStruct(eddy.shape, F32),...]
    unnamed x8 -> x2, local copies, waits for them, and re-layouts: 5.45 us -> 3.49 us
    concatenate x0 -> x1, other arithmetic: none -> 0.76 us  [body(): jnp.concatenate([target_device.reshape(1, 128), target_block.reshape(1, 1...]
where the time goes in v1:
time: 56 us; the launch traced here: 55.9 us
  Pallas kernels  50.3 us (90%)
  local copies, waits for them, and re-layouts  3.56 us (6%)
  between operations  1.29 us (2%)
  other arithmetic  0.76 us (1%)
    pallas_call x1, Pallas kernels, body(): pl.pallas_call(kernel, out_shape=(jax.ShapeDtypeStruct(eddy.shape, F32),...  50.3 us
    unnamed x2, local copies, waits for them, and re-layouts  3.49 us

profile of v1, /device:TPU:0, one launch (start us, length us, event | category | flops | bytes accessed | tf_op | source)
XLA Modules:
  0.0 55.9 jit_solution(11013109694964332760)
XLA Ops:
  1.3 0.1 pad.3.clone
  1.4 0.8 %add_add_fusion.numbers = s32[4,128]{1,0:T(4,128)S(1)} fusion(s32[1,128]{1,0:T(1,128)} %bitcast.9, s32[1,128]{1,0:T(1,128)} %bitcast.10, s32[1,128]{1,0:T(1,128)} %bitcast.11, s32[4]{0:T(128)S(1)} %pad.3.clone), kind=kLoop, calls=%fused_computation | loop fusion | flops 1536 | bytes 3600 | tf_op jit(solution)/shard_map/concatenate | solution.py:642
  2.1 50.3 %jet_step.1 = (f32[5,8,32,256]{3,2,1,0:T(8,128)}, f32[4,16,16,256]{3,2,1,0:T(8,128)S(1)}) custom-call(f32[5,8,32,256]{3,2,1,0:T(8,128)} %eddy.1, f32[4,16,16,256]{3,2,1,0:T(8,128)} %acoustic.1, bf16[128,128,128]{2,1,0:T(8,128)(2,1)} %bitcast.8, s32[4,128]{1,0:T(4,128)S(1)} %add_add_fusion.numbers), custom_call_target="tpu_custom_call" | custom-call | tf_op jit(solution)/shard_map/jet_step/pallas_call | solution.py:650
  52.4 2.5 %copy.12 = f32[5,8,32,256]{3,2,1,0:T(8,128)} copy(f32[5,8,32,256]{3,2,1,0:T(8,128)} %get-tuple-element.4) | data formatting | bytes 2621440
  54.9 1.0 %copy.13 = f32[4,16,16,256]{3,2,1,0:T(8,128)} copy(f32[4,16,16,256]{3,2,1,0:T(8,128)S(1)} %get-tuple-element.5) | data formatting | bytes 2097152

commit v2 on v1

--- a/solution.py
+++ b/solution.py
@@ -142,9 +142,6 @@
     def x_line(k):
         return lax.rem(g + k, GX), r
 
-    small = pltpu.make_async_copy(numbers, numbers_s, small_sem)
-    small.start()
-
     bar = pltpu.get_barrier_semaphore()
     for i, j in CORNERS:
         signal(bar, ((left, right)[i], (below, above)[j]))
@@ -174,25 +171,8 @@
             )
         )
     loads.append(pltpu.make_async_copy(weights, wv, load_sem.at[4]))
-    for copy in loads:
-        copy.start()
-
-    @pl.loop(0, 4)
-    def _(n):
-        @pl.loop(0, 3)
-        def _(x):
-            for c in range(4):
-                for zh in range(2):
-                    for line in (x, x + 19):
-                        for t in (8, 16):
-                            ys[n, c, line, zh, t : t + 8, :] = zero
-
-        @pl.loop(3, 19)
-        def _(x):
-            for c in RADIAL:
-                for zh in range(2):
-                    for t in (0, 24):
-                        ys[n, c, x, zh, t : t + 8, :] = zero
+    loads[0].start()
+    loads[1].start()
 
     @pl.when(r == 0)
     def _():
@@ -202,24 +182,12 @@
     def _():
         f0[:, :, :, 40:48, :] = jnp.zeros((5, 12, 2, 8, 128), F32)
 
-    entry = lax.broadcasted_iota(jnp.int32, (128, 128), 0)
-    device = lax.broadcasted_iota(jnp.int32, (128, 128), 1)
-    named = jnp.broadcast_to(numbers[0:1, :], (128, 128)).T
-    block = jnp.broadcast_to(numbers[1:2, :], (128, 128)).T
-    hit = (named == device) & (entry < numbers[3:4, :])
-    first = jnp.min(jnp.where(hit, entry, 128), axis=0, keepdims=True)
-    last = jnp.max(jnp.where(hit, entry, -1), axis=0, keepdims=True)
-    id_first = jnp.max(jnp.where(hit & (entry == first), block, -1), axis=0, keepdims=True)
-    id_last = jnp.max(jnp.where(hit & (entry == last), block, -1), axis=0, keepdims=True)
-    slots[0:1, :] = jnp.where(first < 128, first, 0)
-    slots[1:2, :] = jnp.maximum(last, 0)
-    lists[me, 0:1, :] = id_first
-    lists[me, 1:2, :] = jnp.where(last > first, id_last, -1)
-    slot_copy = pltpu.make_async_copy(slots, slots_s, slot_sem)
-    slot_copy.start()
-
     loads[0].wait()
     loads[1].wait()
+    small = pltpu.make_async_copy(numbers, numbers_s, small_sem)
+    small.start()
+    for copy in loads[2:]:
+        copy.start()
 
     flat0 = f0.reshape(5 * 12 * 2 * FR, 128)
 
@@ -256,10 +224,50 @@
         flow_copies.append(remote(csend.at[n], crecv.at[n], fc_s.at[n], fc_r.at[n], where))
 
     pl.semaphore_wait(bar, 4 + 2 + 6 + GX - 1)
-    for copy in flow_copies:
+    for copy in flow_copies[2:4] + flow_copies[:2] + flow_copies[4:]:
         copy.start()
     for k in range(1, 4):
         signal(plane_in, y_line(k))
+
+    entry = lax.broadcasted_iota(jnp.int32, (128, 128), 0)
+    device = lax.broadcasted_iota(jnp.int32, (128, 128), 1)
+    named = jnp.broadcast_to(numbers[0:1, :], (128, 128)).T
+    block = jnp.broadcast_to(numbers[1:2, :], (128, 128)).T
+    hit = (named == device) & (entry < numbers[3:4, :])
+    first = jnp.min(jnp.where(hit, entry, 128), axis=0, keepdims=True)
+    last = jnp.max(jnp.where(hit, entry, -1), axis=0, keepdims=True)
+    id_first = jnp.max(jnp.where(hit & (entry == first), block, -1), axis=0, keepdims=True)
+    id_last = jnp.max(jnp.where(hit & (entry == last), block, -1), axis=0, keepdims=True)
+    slots[0:1, :] = jnp.where(first < 128, first, 0)
+    slots[1:2, :] = jnp.maximum(last, 0)
+    lists[me, 0:1, :] = id_first
+    lists[me, 1:2, :] = jnp.where(last > first, id_last, -1)
+    slot_copy = pltpu.make_async_copy(slots, slots_s, slot_sem)
+    slot_copy.start()
+
+    @pl.loop(0, 4)
+    def _(n):
+        @pl.loop(0, 3)
+        def _(x):
+            for c in range(4):
+                for zh in range(2):
+                    for line in (x, x + 19):
+                        for t in (8, 16):
+                            ys[n, c, line, zh, t : t + 8, :] = zero
+
+        @pl.loop(3, 19)
+        def _(x):
+            for c in RADIAL:
+                for zh in range(2):
+                    for t in (0, 24):
+                        ys[n, c, x, zh, t : t + 8, :] = zero
+
+    def clear_flow_rows(low, high):
+        for row, end in ((7, r == 0), (40, r == ROW - 1)):
+
+            @pl.when(end)
+            def _():
+                f1[:, low:high, :, row : row + 1, :] = jnp.zeros((5, high - low, 2, 1, 128), F32)
 
     def first_step(x, tiles):
         for t in tiles:
@@ -304,6 +312,24 @@
     @pl.loop(3, 9, unroll=2)
     def _(x):
         first_step(x, (0, 4))
+
+    def second_step(x):
+        for t in range(4):
+
+            def emit(zh, new):
+                for c in range(5):
+                    f2[c, x, 8 * t : 8 * t + 8, 128 * zh : 128 * zh + 128] = new[c]
+                rho = 1.0 + new[0]
+                for c, value in enumerate((new[4], rho * new[1], rho * new[2], rho * new[3])):
+                    srcs[pl.ds(8 + x * 256 + 64 * t + 4 * zh + c, 8, stride=8), :] = value
+
+            flow_tile(f1, x + 1, 8 + 8 * t, lane, emit)
+
+    clear_flow_rows(2, 8)
+
+    @pl.loop(2, 6, unroll=2)
+    def _(x):
+        second_step(x)
 
     for copy in flow_copies[2:]:
         copy.wait_recv()
@@ -376,26 +402,12 @@
     def _():
         f1[:, 9, :, :, :] = jnp.zeros((5, 2, FR, 128), F32)
 
-    @pl.when(r == 0)
-    def _():
-        f1[:, :, :, 7:8, :] = jnp.zeros((5, 10, 2, 1, 128), F32)
-
-    @pl.when(r == ROW - 1)
-    def _():
-        f1[:, :, :, 40:41, :] = jnp.zeros((5, 10, 2, 1, 128), F32)
-
-    @pl.loop(0, 8, unroll=2)
-    def _(x):
-        for t in range(4):
-
-            def emit(zh, new):
-                for c in range(5):
-                    f2[c, x, 8 * t : 8 * t + 8, 128 * zh : 128 * zh + 128] = new[c]
-                rho = 1.0 + new[0]
-                for c, value in enumerate((new[4], rho * new[1], rho * new[2], rho * new[3])):
-                    srcs[pl.ds(8 + x * 256 + 64 * t + 4 * zh + c, 8, stride=8), :] = value
-
-            flow_tile(f1, x + 1, 8 + 8 * t, lane, emit)
+    clear_flow_rows(1, 2)
+    clear_flow_rows(8, 9)
+
+    @pl.loop(0, 4, unroll=2)
+    def _(n):
+        second_step(n + 4 * lax.div(n, 2))
 
     flow_out = pltpu.make_async_copy(f2, eddy_out, out_sem)
     flow_out.start()
@@ -410,7 +422,7 @@
     loads[4].wait()
     small.wait()
 
-    @pl.loop(0, 8)
+    @pl.loop(0, 8, unroll=2)
     def _(m):
         for u in range(8):
             p = m * 8 + u
@@ -431,7 +443,7 @@
         high = contrib[pl.ds(4 + 4 * jnp.clip(slots_s[1, d], 0, 127), 8), :]
         return jnp.where(sub < 4, low, high)
 
-    @pl.loop(1, DEV)
+    @pl.loop(1, DEV, unroll=6)
     def _(k):
         d = lax.rem(me + k, DEV)
         outgoing[d] = slot_tile(d)
@@ -603,20 +615,18 @@
         high = value.astype(jnp.bfloat16)
         low = (value - high.astype(F32)).astype(jnp.bfloat16)
 
-        @pl.loop(0, 4)
-        def _(q):
-            rows = onehot[pl.ds(pl.multiple_of(q * 128, 128), 128), :]
-            total = jnp.dot(rows, high, preferred_element_type=F32) + jnp.dot(
-                rows, low, preferred_element_type=F32
-            )
-            for c in range(2):
-                part = total[:, 128 * c : 128 * c + 128]
-                source[2 * pair + c, pl.ds(pl.multiple_of(q * 128, 128), 128), :] = part
-                for i in range(4):
-                    for zh in range(2):
-                        at = (1, 2 * pair + c, q * 4 + i + 3, zh, points, slice(None))
-                        piece = part[32 * i + 16 * zh : 32 * i + 16 * zh + 16, :]
-                        ys[at] = ys[at] + (sound_timestep / 4.0) * piece
+        rows = onehot[...]
+        total = jnp.dot(rows, high, preferred_element_type=F32) + jnp.dot(
+            rows, low, preferred_element_type=F32
+        )
+        for c in range(2):
+            part = total[:, 128 * c : 128 * c + 128]
+            source[2 * pair + c] = part
+            for x in range(16):
+                for zh in range(2):
+                    at = (1, 2 * pair + c, x + 3, zh, points, slice(None))
+                    piece = part[32 * x + 16 * zh : 32 * x + 16 * zh + 16, :]
+                    ys[at] = ys[at] + (sound_timestep / 4.0) * piece
 
     acoustic_pack(1)
     for n in range(1, 4):

time: 56 us -> 53.8 us (0.961)
  Pallas kernels: 50.3 us -> 48 us
    pallas_call x1, Pallas kernels: 50.3 us -> 48 us  [body(): pl.pallas_call(kernel, out_shape=(jax.ShapeDtypeStruct(eddy.shape, F32),...]
where the time goes in v2:
time: 53.8 us; the launch traced here: 53.6 us
  Pallas kernels  48 us (89%)
  local copies, waits for them, and re-layouts  3.56 us (7%)
  between operations  1.29 us (2%)
  other arithmetic  0.76 us (1%)
    pallas_call x1, Pallas kernels, body(): pl.pallas_call(kernel, out_shape=(jax.ShapeDtypeStruct(eddy.shape, F32),...  48 us
    unnamed x2, local copies, waits for them, and re-layouts  3.49 us

profile of v2, /device:TPU:0, one launch (start us, length us, event | category | flops | bytes accessed | tf_op | source)
XLA Modules:
  0.0 53.6 jit_solution(18296175838893112610)
XLA Ops:
  1.3 0.1 pad.3.clone
  1.4 0.8 %add_add_fusion.numbers = s32[4,128]{1,0:T(4,128)S(1)} fusion(s32[1,128]{1,0:T(1,128)} %bitcast.9, s32[1,128]{1,0:T(1,128)} %bitcast.10, s32[1,128]{1,0:T(1,128)} %bitcast.11, s32[4]{0:T(128)S(1)} %pad.3.clone), kind=kLoop, calls=%fused_computation | loop fusion | flops 1536 | bytes 3600 | tf_op jit(solution)/shard_map/concatenate | solution.py:652
  2.1 48.0 %jet_step.1 = (f32[5,8,32,256]{3,2,1,0:T(8,128)}, f32[4,16,16,256]{3,2,1,0:T(8,128)S(1)}) custom-call(f32[5,8,32,256]{3,2,1,0:T(8,128)} %eddy.1, f32[4,16,16,256]{3,2,1,0:T(8,128)} %acoustic.1, bf16[128,128,128]{2,1,0:T(8,128)(2,1)} %bitcast.8, s32[4,128]{1,0:T(4,128)S(1)} %add_add_fusion.numbers), custom_call_target="tpu_custom_call" | custom-call | tf_op jit(solution)/shard_map/jet_step/pallas_call | solution.py:660
  50.1 2.5 %copy.12 = f32[5,8,32,256]{3,2,1,0:T(8,128)} copy(f32[5,8,32,256]{3,2,1,0:T(8,128)} %get-tuple-element.4) | data formatting | bytes 2621440
  52.6 1.0 %copy.13 = f32[4,16,16,256]{3,2,1,0:T(8,128)} copy(f32[4,16,16,256]{3,2,1,0:T(8,128)S(1)} %get-tuple-element.5) | data formatting | bytes 2097152

commit v3 on v2

--- a/solution.py
+++ b/solution.py
@@ -186,8 +186,6 @@
     loads[1].wait()
     small = pltpu.make_async_copy(numbers, numbers_s, small_sem)
     small.start()
-    for copy in loads[2:]:
-        copy.start()
 
     flat0 = f0.reshape(5 * 12 * 2 * FR, 128)
 
@@ -225,6 +223,8 @@
 
     pl.semaphore_wait(bar, 4 + 2 + 6 + GX - 1)
     for copy in flow_copies[2:4] + flow_copies[:2] + flow_copies[4:]:
+        copy.start()
+    for copy in loads[2:]:
         copy.start()
     for k in range(1, 4):
         signal(plane_in, y_line(k))

time: 53.8 us -> 53.8 us (level)
  no operation moved by 1% of the time
where the time goes in v3:
time: 53.8 us; the launch traced here: 53.6 us
  Pallas kernels  48 us (89%)
  local copies, waits for them, and re-layouts  3.56 us (7%)
  between operations  1.29 us (2%)
  other arithmetic  0.76 us (1%)
    pallas_call x1, Pallas kernels, body(): pl.pallas_call(kernel, out_shape=(jax.ShapeDtypeStruct(eddy.shape, F32),...  48 us
    unnamed x2, local copies, waits for them, and re-layouts  3.49 us

profile of v3, /device:TPU:0, one launch (start us, length us, event | category | flops | bytes accessed | tf_op | source)
XLA Modules:
  0.0 53.6 jit_solution(3749308828913854094)
XLA Ops:
  1.3 0.1 pad.3.clone
  1.4 0.8 %add_add_fusion.numbers = s32[4,128]{1,0:T(4,128)S(1)} fusion(s32[1,128]{1,0:T(1,128)} %bitcast.9, s32[1,128]{1,0:T(1,128)} %bitcast.10, s32[1,128]{1,0:T(1,128)} %bitcast.11, s32[4]{0:T(128)S(1)} %pad.3.clone), kind=kLoop, calls=%fused_computation | loop fusion | flops 1536 | bytes 3600 | tf_op jit(solution)/shard_map/concatenate | solution.py:652
  2.1 48.0 %jet_step.1 = (f32[5,8,32,256]{3,2,1,0:T(8,128)}, f32[4,16,16,256]{3,2,1,0:T(8,128)S(1)}) custom-call(f32[5,8,32,256]{3,2,1,0:T(8,128)} %eddy.1, f32[4,16,16,256]{3,2,1,0:T(8,128)} %acoustic.1, bf16[128,128,128]{2,1,0:T(8,128)(2,1)} %bitcast.8, s32[4,128]{1,0:T(4,128)S(1)} %add_add_fusion.numbers), custom_call_target="tpu_custom_call" | custom-call | tf_op jit(solution)/shard_map/jet_step/pallas_call | solution.py:660
  50.1 2.5 %copy.12 = f32[5,8,32,256]{3,2,1,0:T(8,128)} copy(f32[5,8,32,256]{3,2,1,0:T(8,128)} %get-tuple-element.4) | data formatting | bytes 2621440
  52.6 1.0 %copy.13 = f32[4,16,16,256]{3,2,1,0:T(8,128)} copy(f32[4,16,16,256]{3,2,1,0:T(8,128)S(1)} %get-tuple-element.5) | data formatting | bytes 2097152
